TPU v7x, 128 devices: a whole 4x4x4 slice. The times are simulated.
128 devices in a mesh: mem: 4 (over x_hi, core), pts: 32 (over x_lo, y, z).
Axes of the slice: x: 4 (x_hi: 2, x_lo: 2; x = x_hi * 2 + x_lo), y: 4, z: 4, core: 2. Of those that a mesh axis runs over, the one named last changes fastest.
Arguments:
- latent: bfloat16 [8, 65536, 1024], P('mem', 'pts'), may hold values from -6 to 6
- head_weight: bfloat16 [102, 1024], replicated, may hold values from -0.1875 to 0.1875
- head_bias: bfloat16 [102], replicated, may hold values from -3 to 3
- targets: float32 [102, 65536], P(None, 'pts'), may hold values from -6 to 6
- cell_area: float32 [65536], P('pts'), may hold values from 0.3 to 3
- field_level: int32 [102], replicated, may hold values from 0 to 12
- source: int32 [65536], P('pts'), may hold values from 0 to 65535, as said below
Outputs:
- latent_grad: bfloat16 [8, 65536, 1024], P('mem', 'pts')
- weight_grad: float32 [102, 1024], replicated
- bias_grad: float32 [102], replicated
Inputs may be any that keep to these rules, and one draw needn't show every extreme that they name: source is a permutation of the grid points; slot s of the block of 2048 slots of pts index j (s counted from 0 inside the block) holds a point of the grid block of pts index s mod (32), that is, a grid index in that block's range of 2048 indices.
All inputs are finite; a program needn't handle non-finite values.
Results may differ from a plain program's by a relative error of at most 0.0085.
Values may be sent and summed in bfloat16 or wider, within the bound.
A program may use at most 64 MiB of HBM per device.

v0:
```python
import jax
import jax.numpy as jnp
from jax import lax
from jax.experimental import pallas as pl
from jax.experimental.pallas import tpu as pltpu
from jax.sharding import PartitionSpec as P

M = 8
F = 102
L = 1024
FP = 104
FB = 112
MAIN = 96
SLOTS = 2048
HALF = 1024
CH = 256
NK = HALF // CH
ROWS = 208
PTS = 32
GROUP = 64
TILE = 16
WIDE = L // 2
TILES = (FB // TILE) * (WIDE // 128)
CHIPS = 64
VMEM = 40 * 2**20
EARLY = 2
ORDER = (0, 2, 1, 3)
MESH = pl.DeviceIdType.MESH

FAIR_ALPHA = 0.95
SMOOTH_WIDTH = 0.25
SPREAD = (1.0 - (1.0 - FAIR_ALPHA) / M) / (M - 1)


def smooth_sign(diff):
    return diff * lax.rsqrt(diff * diff + SMOOTH_WIDTH * SMOOTH_WIDTH)


def pair_sums(own, far):
    spread = [None] * len(own)

    def add(at, term):
        spread[at] = term if spread[at] is None else spread[at] + term

    for a in range(len(own)):
        for b in range(a + 1, len(own)):
            q = smooth_sign(own[a] - own[b])
            add(a, q)
            add(b, -q)
        for other in far:
            add(a, smooth_sign(own[a] - other))
    return spread


def gradients(own, spread, target, scale):
    return [
        (scale * (smooth_sign(value - target) - SPREAD * others)).astype(jnp.bfloat16)
        for value, others in zip(own, spread, strict=True)
    ]


def column(row, rows):
    n = row.shape[1]
    at = lax.broadcasted_iota(jnp.int32, (rows, n), 0)
    lane = lax.broadcasted_iota(jnp.int32, (rows, n), 1)
    return jnp.sum(jnp.where(at == lane, row, 0.0), axis=1, keepdims=True)


def main_kernel(
    latent, w_hbm, bias_hbm, level_hbm, tgt, area_hbm, src_hbm,
    lg, ag,
    lat, w_ref, bias_ref, level_ref, area_ref, src_ref,
    wpad, tv, tt, last8, asked, tq, rq, tslot, bcol, wcol,
    psend, pmate, prem, gl, gx, mlat, acc, bsum, rs, accb, sent, sp,
    lat_sem, small_sem, tgt_sem, ask_s, ask_r, tq_s, tq_r,
    ps_far, pr_far, ps_mate, pr_mate, ms, mr, gs, gr, ar_s, ar_r,
):
    i = lax.axis_index("mem")
    pts = lax.axis_index("pts")
    xh = lax.div(i, 2)
    c = lax.rem(i, 2)
    xl = lax.div(pts, 16)
    me = xh * PTS + pts
    mate = (xh * 2 + (1 - c), pts)
    far = ((1 - xh) * 2 + c, pts)
    far_mate = ((1 - xh) * 2 + (1 - c), pts)
    halves = (c, 1 - c)

    def lat_copy(e, k):
        off = pl.multiple_of(halves[e] * HALF + k * CH, CH)
        return pltpu.make_async_copy(
            latent.at[:, pl.ds(off, CH)], lat.at[e, k], lat_sem.at[e * NK + k]
        )

    small = [
        pltpu.make_async_copy(src, dst, small_sem.at[n])
        for n, (src, dst) in enumerate(
            (
                (w_hbm, w_ref), (bias_hbm, bias_ref), (level_hbm, level_ref),
                (area_hbm, area_ref), (src_hbm, src_ref),
            )
        )
    ]
    tgt_copy = pltpu.make_async_copy(tgt, tv, tgt_sem)
    for copy in small:
        copy.start()
    for k in range(NK):
        for e in range(2):
            lat_copy(e, k).start()
        if k == 0:
            tgt_copy.start()

    barrier = pltpu.get_barrier_semaphore()

    def group_device(n):
        q = lax.rem(me + n, GROUP)
        q_xh = lax.div(q, PTS)
        q_pts = lax.rem(q, PTS)
        return q, q_xh, q_pts, (q_xh * 2 + c, q_pts)

    pl.semaphore_signal(barrier, inc=1, device_id=far_mate, device_id_type=MESH)
    pl.semaphore_signal(barrier, inc=1, device_id=mate, device_id_type=MESH)

    def greet(n, _):
        pl.semaphore_signal(barrier, inc=1, device_id=group_device(n)[3], device_id_type=MESH)
        return 0

    lax.fori_loop(1, GROUP, greet, 0)

    for copy in small:
        copy.wait()
    wpad[...] = jnp.zeros_like(wpad)
    wpad[0:F, :] = w_ref[...]
    bcol[...] = jnp.broadcast_to(column(bias_ref[...].astype(jnp.float32), FP), bcol.shape)
    level = (level_ref[...].astype(jnp.float32) + 1.0) / 7.0
    wcol[...] = jnp.broadcast_to(column(level, FP), wcol.shape)
    acc[...] = jnp.zeros_like(acc)
    bsum[...] = jnp.zeros_like(bsum)

    def far_copy(e, k):
        return pltpu.make_async_remote_copy(
            src_ref=psend.at[e, k],
            dst_ref=prem.at[e, k],
            send_sem=ps_far.at[e * NK + k],
            recv_sem=pr_far.at[e * NK + k],
            device_id=far if e == 0 else far_mate,
            device_id_type=MESH,
        )

    def mate_copy(k):
        return pltpu.make_async_remote_copy(
            src_ref=psend.at[1, k],
            dst_ref=pmate.at[k],
            send_sem=ps_mate.at[k],
            recv_sem=pr_mate.at[k],
            device_id=mate,
            device_id_type=MESH,
        )

    def predict(e, k):
        lat_copy(e, k).wait()
        rest = []
        for m in range(2):
            pred = lax.dot_general(
                wpad[...], lat[e, k, m], (((1,), (1,)), ((), ())),
                preferred_element_type=jnp.float32,
            )[0:FP]
            pred = pred + bcol[:, 0:1]
            psend[e, k, m * MAIN : (m + 1) * MAIN, :] = pred[0:MAIN].astype(jnp.bfloat16)
            rest.append(pred[MAIN:FP])
        psend[e, k, 2 * MAIN :, :] = jnp.concatenate(rest, axis=0).astype(jnp.bfloat16)

    def send(e, k):
        far_copy(e, k).start()
        if e == 1:
            mate_copy(k).start()

    for e in range(2):
        predict(e, 0)

    pl.semaphore_wait(barrier, GROUP + 1)

    def owner_of(n):
        p = lax.rem(pts + n, PTS)
        differ = lax.rem(lax.div(p, 16) + xl, 2)
        return p, (lax.rem(xh + c * differ, 2) * 2 + c, p)

    def across_first(n):
        return 1 + lax.rem(n + 14, PTS - 1)

    def ask(n, _):
        pltpu.make_async_remote_copy(
            src_ref=src_ref.at[pl.ds(pl.multiple_of(8 * c, 8), 8)],
            dst_ref=asked.at[pts],
            send_sem=ask_s,
            recv_sem=ask_r,
            device_id=owner_of(across_first(n))[1],
            device_id_type=MESH,
        ).start()
        return 0

    lax.fori_loop(1, PTS, ask, 0)
    for e in range(2):
        send(e, 0)

    asked[pts] = src_ref[pl.ds(pl.multiple_of(8 * c, 8), 8), :]

    for k in range(1, NK):
        for e in range(2):
            predict(e, k)

    def lend(e, k):
        lanes = pl.ds(pl.multiple_of((1 - c) * WIDE, WIDE), WIDE)
        return pltpu.make_async_remote_copy(
            src_ref=lat.at[e, k, :, :, lanes],
            dst_ref=mlat.at[1 - e, k],
            send_sem=ms.at[e * NK + k],
            recv_sem=mr.at[(1 - e) * NK + k],
            device_id=mate,
            device_id_type=MESH,
        )

    def lent(e, k):
        return pltpu.make_async_copy(mlat.at[e, k], mlat.at[e, k], mr.at[e * NK + k])

    for e in range(2):
        lend(e, 0).start()

    tgt_copy.wait()
    tt[FP:128, :] = jnp.zeros((128 - FP, SLOTS), jnp.bfloat16)
    tt[128 + FP :, :] = jnp.zeros((128 - FP, SLOTS), jnp.bfloat16)
    last8[...] = jnp.zeros_like(last8)
    last8[0 : F - MAIN, :] = tv[MAIN:F, :]
    last8[F - MAIN : F - MAIN + 1, :] = area_ref[...]

    def split(value, at):
        high = value.astype(jnp.bfloat16)
        tt[at : at + value.shape[0], :] = high
        low = (value - high.astype(jnp.float32)).astype(jnp.bfloat16)
        tt[128 + at : 128 + at + value.shape[0], :] = low

    for at in range(0, MAIN, 32):
        split(tv[at : at + 32, :], at)
    split(last8[...], MAIN)


    def asked_bytes(sem):
        return pltpu.make_async_copy(
            asked.at[pl.ds(0, PTS - 1)], asked.at[pl.ds(0, PTS - 1)], sem
        )

    asked_bytes(ask_r).wait()
    for e in range(2):
        send(e, 1)
    found = asked[...].reshape(PTS * 8, 128) - pts * SLOTS
    lane = lax.broadcasted_iota(jnp.int32, (PTS * 8, 128), 1)
    row = lax.broadcasted_iota(jnp.int32, (PTS * 8, 128), 0)
    found = jnp.where(lax.rem(lane, 32) == pts, found, 0)
    spread_row = lax.broadcasted_iota(jnp.int32, (128, 128), 0)
    spread_lane = lax.broadcasted_iota(jnp.int32, (128, 128), 1)
    spread = jnp.where(lax.div(spread_row, 32) == lax.div(spread_lane, 32), 1.0, 0.0)
    spread = spread.astype(jnp.bfloat16)
    high = lax.shift_right_logical(found, 6).astype(jnp.float32).astype(jnp.bfloat16)
    low = lax.bitwise_and(found, 63).astype(jnp.float32).astype(jnp.bfloat16)
    wide = 64.0 * jnp.dot(high, spread, preferred_element_type=jnp.float32) + jnp.dot(
        low, spread, preferred_element_type=jnp.float32
    )
    wide = jnp.where(lax.rem(lane, 32) == lax.rem(row, 32), wide, 0.0)
    wanted = jnp.sum(wide.reshape(8, 32, 128), axis=1)
    for half in range(4):
        cols = jnp.concatenate(
            [column(wanted[2 * half + b : 2 * half + b + 1, :], 128) for b in range(2)], axis=0
        ).astype(jnp.int32)
        place = lax.broadcasted_iota(jnp.int32, (256, SLOTS), 1)
        onehot = jnp.where(place == cols, 1.0, 0.0).astype(jnp.bfloat16)
        got = lax.dot_general(
            onehot, tt[...], (((1,), (1,)), ((), ())), preferred_element_type=jnp.float32
        )
        got = got[:, 0:128] + got[:, 128:256]
        tq[2 * half : 2 * half + 2] = got.reshape(2, 4, 4, 8, 128)

    def answer(n, _):
        p, device = owner_of(across_first(n))
        pltpu.make_async_remote_copy(
            src_ref=tq.at[lax.div(p, 4), :, lax.rem(p, 4)],
            dst_ref=rq.at[:, pts],
            send_sem=tq_s,
            recv_sem=tq_r,
            device_id=device,
            device_id_type=MESH,
        ).start()
        return 0

    lax.fori_loop(1, PTS, answer, 0)
    rq[:, pts] = tq[lax.div(pts, 4), :, lax.rem(pts, 4)]

    for k in range(2, NK):
        for e in range(2):
            send(e, k)
    for k in range(1, NK):
        for e in range(2):
            lend(e, k).start()

    def grad_copy(k):
        return pltpu.make_async_remote_copy(
            src_ref=gl.at[k],
            dst_ref=gx.at[k],
            send_sem=gs.at[k],
            recv_sem=gr.at[k],
            device_id=mate,
            device_id_type=MESH,
        )

    def near_buffers(k):
        return psend.at[0, k], pmate.at[k]

    def far_buffers(k):
        return prem.at[0, k], prem.at[1, k]

    def main_rows(buffers, t, lanes):
        return [
            buffer[pl.ds(pl.multiple_of(m * MAIN + 16 * t, 16), 16), lanes].astype(jnp.float32)
            for m in range(2)
            for buffer in buffers
        ]

    def rest_rows(buffers, lanes):
        rest = [buffer[2 * MAIN : ROWS, lanes].astype(jnp.float32) for buffer in buffers]
        return [value[8 * m : 8 * m + 8] for m in range(2) for value in rest]

    def blocks(k):
        for part in range(CH // 128):
            yield slice(128 * part, 128 * (part + 1)), k * CH + 128 * part

    def pairs_chunk(k):
        mate_copy(k).wait_recv()
        far_copy(0, k).wait_recv()
        far_copy(1, k).wait_recv()
        for lanes, at in blocks(k):

            def step(t, _):
                sums = pair_sums(
                    main_rows(near_buffers(k), t, lanes), main_rows(far_buffers(k), t, lanes)
                )
                for n in range(4):
                    sp[n, pl.ds(pl.multiple_of(16 * t, 16), 16), at : at + 128] = sums[n]
                return 0

            lax.fori_loop(0, MAIN // 16, step, 0)
            sums = pair_sums(rest_rows(near_buffers(k), lanes), rest_rows(far_buffers(k), lanes))
            for n in range(4):
                sp[n, MAIN:FP, at : at + 128] = sums[n]

    def grads_chunk(k):
        for lanes, at in blocks(k):

            def grads_of(own, rows):
                return gradients(
                    own, [sp[n, rows, at : at + 128] for n in range(4)],
                    tslot[rows, at : at + 128], wcol[rows, :] * tslot[F : F + 1, at : at + 128],
                )

            def step(t, _):
                rows = pl.ds(pl.multiple_of(16 * t, 16), 16)
                grads = grads_of(main_rows(near_buffers(k), t, lanes), rows)
                for n in range(4):
                    gl[k, ORDER[n], rows, lanes] = grads[n]
                bsum[rows, :] += sum(grad.astype(jnp.float32) for grad in grads)
                return 0

            lax.fori_loop(0, MAIN // 16, step, 0)
            grads = grads_of(rest_rows(near_buffers(k), lanes), slice(MAIN, FP))
            none = jnp.zeros((8, 128), jnp.float32)
            for n in range(4):
                full = jnp.concatenate([grads[n].astype(jnp.float32), none], axis=0)
                gl[k, ORDER[n], MAIN:FB, lanes] = full.astype(jnp.bfloat16)
            bsum[MAIN:FP, :] += sum(grad.astype(jnp.float32) for grad in grads)

    def own_grads(e, k, m):
        return gl[k, m] if e == 0 else gx[k, 2 + m]

    def latent_grad(e, k):
        for m in range(2):
            part = pl.ds(pl.multiple_of(halves[e] * HALF + k * CH, CH), CH)
            lg[m, part, :] = lax.dot_general(
                own_grads(e, k, m), wpad[...], (((0,), (0,)), ((), ())),
                preferred_element_type=jnp.float32,
            ).astype(jnp.bfloat16)

    def accumulate(e, k):
        lent(e, k).wait()
        lanes = pl.ds(pl.multiple_of(c * WIDE, WIDE), WIDE)
        for m in range(2):
            own, other = (gl[k, m], gl[k, 2 + m]) if e == 0 else (gx[k, 2 + m], gx[k, m])
            acc[...] += jnp.dot(
                own, lat[e, k, m, :, lanes], preferred_element_type=jnp.float32
            ) + jnp.dot(other, mlat[e, k, m], preferred_element_type=jnp.float32)

    for k in range(EARLY):
        pairs_chunk(k)

    def rq_bytes(sem):
        return pltpu.make_async_copy(
            rq.at[:, pl.ds(0, PTS - 1)], rq.at[:, pl.ds(0, PTS - 1)], sem
        )

    rq_bytes(tq_r).wait()
    for r in range(8):
        rows = jnp.concatenate([rq[a, :, r, :] for a in range(4)], axis=0)
        tslot[:, 128 * r : 128 * (r + 1)] = rows.T[0:FP]

    for k in range(NK):
        if k >= EARLY:
            pairs_chunk(k)
        grads_chunk(k)
        grad_copy(k).start()
        accumulate(0, k)
        if k > 0:
            grad_copy(k - 1).wait_recv()
            accumulate(1, k - 1)
    grad_copy(NK - 1).wait_recv()
    accumulate(1, NK - 1)

    at = lax.broadcasted_iota(jnp.int32, (FP, 128), 0)
    lane_at = lax.broadcasted_iota(jnp.int32, (FP, 128), 1)
    bias = jnp.sum(bsum[...], axis=1, keepdims=True)
    bias = jnp.sum(jnp.where(at == lane_at, bias, 0.0), axis=0, keepdims=True)
    acc[MAIN:FP, 0:128] += jnp.where(at[0 : FP - MAIN] == F - MAIN, bias, 0.0)
    y = lax.rem(lax.div(pts, 4), 4)
    z = lax.rem(pts, 4)
    x = xh * 2 + xl
    slot = z * 16 + y * 4 + x

    def tile_at(q_xh, q_y, q_z):
        full = lax.div(q_z, 3) * lax.div(q_y, 2) == 0
        return q_z * 8 + q_y * 2 + q_xh, full, lax.rem(c + q_y + q_z, 2)

    tile, full, tile_xl = tile_at(xh, y, z)
    owns = jnp.logical_and(full, tile_xl == xl)

    def acc_tile(q):
        rows = pl.ds(pl.multiple_of(lax.div(q, 4) * TILE, TILE), TILE)
        return rows, pl.ds(pl.multiple_of(lax.rem(q, 4) * 128, 128), 128)

    ys = [lax.rem(y + d, 4) for d in range(4)]
    xs = [lax.rem(x + d, 4) for d in range(4)]
    far_first = (2, 1, 3, 0)

    def scatter(n, _):
        q_z = lax.rem(z + n + 2, 4)
        for dy in far_first:
            for q_xh in (1 - xh, xh):
                q, q_full, q_xl = tile_at(q_xh, ys[dy], q_z)
                there = q_full
                if dy == 0 and q_xh is xh:
                    there = jnp.logical_and(there, jnp.logical_or(n != 2, q_xl != xl))

                @pl.when(there)
                def _(q=q, q_xh=q_xh, q_xl=q_xl, dy=dy):
                    rows, lanes = acc_tile(q)
                    pltpu.make_async_remote_copy(
                        src_ref=accb.at[rows, lanes], dst_ref=rs.at[slot], send_sem=ar_s.at[0],
                        recv_sem=ar_r.at[0],
                        device_id=(q_xh * 2 + c, q_xl * 16 + ys[dy] * 4 + q_z),
                        device_id_type=MESH,
                    ).start()

        return 0

    accb[...] = acc[...].astype(jnp.bfloat16)
    lax.fori_loop(0, 4, scatter, 0)
    for e in range(2):
        for k in range(NK):
            latent_grad(e, k)

    def tiles(ref, count, sem):
        return pltpu.make_async_copy(ref.at[pl.ds(0, count)], ref.at[pl.ds(0, count)], sem)

    @pl.when(owns)
    def _():
        rows, lanes = acc_tile(tile)
        rs[slot] = accb[rows, lanes]
        tiles(rs, CHIPS - 1, ar_r.at[0]).wait()
        mine = c * TILES + tile
        ag[mine] = jnp.sum(rs[...].astype(jnp.float32), axis=0).astype(jnp.bfloat16)

        def share(device):
            pltpu.make_async_remote_copy(
                src_ref=ag.at[mine], dst_ref=ag.at[mine], send_sem=ar_s.at[1],
                recv_sem=ar_r.at[1], device_id=device, device_id_type=MESH,
            ).start()

        def gather(n, _):
            q_z = lax.rem(z + n + 2, 4)

            def chip(dy, dx):
                q_mem = lax.div(xs[dx], 2) * 2
                q_pts = lax.rem(xs[dx], 2) * 16 + ys[dy] * 4 + q_z
                for core in range(2):
                    share((q_mem + core, q_pts))

            for dy in far_first:
                for dx in far_first:
                    if dy == 0 and dx == 0:
                        pl.when(n != 2)(lambda: chip(0, 0))
                    else:
                        chip(dy, dx)
            return 0

        lax.fori_loop(0, 4, gather, 0)
        share(mate)

    for k in range(NK):
        for e in range(2):
            far_copy(e, k).wait_send()
            lend(e, k).wait_send()
        mate_copy(k).wait_send()
        grad_copy(k).wait_send()
    asked_bytes(ask_s).wait()
    rq_bytes(tq_s).wait()

    @pl.when(owns)
    def _():
        tiles(rs, TILES - 1, ar_s.at[0]).wait()
        tiles(ag, 2 * TILES - 1, ar_r.at[1]).wait()
        tiles(sent, 2 * CHIPS - 1, ar_s.at[1]).wait()

    @pl.when(jnp.logical_not(owns))
    def _():
        tiles(rs, TILES, ar_s.at[0]).wait()
        tiles(ag, 2 * TILES, ar_r.at[1]).wait()


def output_kernel(lg, ag, lg_out, wg_out, bg_out, wg, bg, sem):
    norm = float(M * SLOTS * PTS) ** (-0.5)
    parts = 4
    size = SLOTS // parts
    copies = [
        pltpu.make_async_copy(
            lg.at[m, pl.ds(size * n, size)], lg_out.at[m, pl.ds(size * n, size)],
            sem.at[parts * m + n],
        )
        for m in range(2) for n in range(parts)
    ]
    for copy in copies:
        copy.start()
    for q in range(2 * TILES):
        t, lb = q % TILES // 4, q // TILES * 4 + q % 4
        rows = min(F, TILE * (t + 1)) - TILE * t
        tile_sum = ag[q].astype(jnp.float32) * norm
        wg[TILE * t : TILE * t + rows, 128 * lb : 128 * (lb + 1)] = tile_sum[0:rows]
    last = MAIN // TILE * 4
    pair = ag[last].astype(jnp.float32) + ag[TILES + last].astype(jnp.float32)
    bg[...] = pair[F - MAIN : F - MAIN + 1, 0:F] * norm
    for n, (src, dst) in enumerate(((wg, wg_out), (bg, bg_out))):
        copies.append(pltpu.make_async_copy(src, dst, sem.at[2 * parts + n]))
        copies[-1].start()
    for copy in copies:
        copy.wait()


def per_device(latent, head_weight, head_bias, targets, cell_area, field_level, source):
    vmem = pl.BlockSpec(memory_space=pltpu.VMEM)
    hbm = pl.BlockSpec(memory_space=pltpu.HBM)
    bf16, f32 = jnp.bfloat16, jnp.float32
    dma = pltpu.SemaphoreType.DMA
    operands = (
        latent, head_weight, head_bias.reshape(1, F), field_level.reshape(1, F), targets,
        cell_area.reshape(1, SLOTS), source.reshape(16, 128),
    )
    latents, sums = pl.pallas_call(
        main_kernel,
        out_shape=(
            pltpu.VMEM((2, SLOTS, L), bf16),
            pltpu.VMEM((2 * TILES, TILE, 128), bf16),
        ),
        in_specs=[hbm] * 7,
        out_specs=(vmem, vmem),
        scratch_shapes=[
            pltpu.VMEM((2, NK, 2, CH, L), bf16),
            pltpu.VMEM((F, L), bf16),
            pltpu.VMEM((1, F), bf16),
            pltpu.VMEM((1, F), jnp.int32),
            pltpu.VMEM((1, SLOTS), f32),
            pltpu.VMEM((16, 128), jnp.int32),
            pltpu.VMEM((FB, L), bf16),
            pltpu.VMEM((F, SLOTS), f32),
            pltpu.VMEM((256, SLOTS), bf16),
            pltpu.VMEM((8, SLOTS), f32),
            pltpu.VMEM((PTS, 8, 128), jnp.int32),
            pltpu.VMEM((8, 4, 4, 8, 128), f32),
            pltpu.VMEM((4, PTS, 8, 128), f32),
            pltpu.VMEM((FP, HALF), f32),
            pltpu.VMEM((FP, 128), f32),
            pltpu.VMEM((FP, 128), f32),
            pltpu.VMEM((2, NK, ROWS, CH), bf16),
            pltpu.VMEM((NK, ROWS, CH), bf16),
            pltpu.VMEM((2, NK, ROWS, CH), bf16),
            pltpu.VMEM((NK, 4, FB, CH), bf16),
            pltpu.VMEM((NK, 4, FB, CH), bf16),
            pltpu.VMEM((2, NK, 2, CH, WIDE), bf16),
            pltpu.VMEM((FB, WIDE), f32),
            pltpu.VMEM((FP, 128), f32),
            pltpu.VMEM((CHIPS, TILE, 128), bf16),
            pltpu.VMEM((FB, WIDE), bf16),
            pltpu.VMEM((2 * CHIPS, TILE, 128), bf16),
            pltpu.VMEM((4, FP, HALF), f32),
            dma((2 * NK,)),
            dma((5,)),
            dma,
            dma, dma, dma, dma,
            dma((2 * NK,)), dma((2 * NK,)),
            dma((NK,)), dma((NK,)),
            dma((2 * NK,)), dma((2 * NK,)),
            dma((NK,)), dma((NK,)),
            dma((2,)), dma((2,)),
        ],
        compiler_params=pltpu.CompilerParams(
            collective_id=0, has_side_effects=True, vmem_limit_bytes=VMEM
        ),
    )(*(pltpu.with_memory_space_constraint(x, pltpu.HBM) for x in operands))
    latent_grad, weight_grad, bias_grad = pl.pallas_call(
        output_kernel,
        in_specs=[vmem, vmem],
        out_specs=(hbm, hbm, hbm),
        out_shape=(
            jax.ShapeDtypeStruct((2, SLOTS, L), bf16),
            jax.ShapeDtypeStruct((F, L), f32),
            jax.ShapeDtypeStruct((1, F), f32),
        ),
        scratch_shapes=[pltpu.VMEM((F, L), f32), pltpu.VMEM((1, F), f32), dma((10,))],
        compiler_params=pltpu.CompilerParams(vmem_limit_bytes=8 * 2**20),
    )(latents, sums)
    return latent_grad, weight_grad, bias_grad.reshape(F)


def solution(mesh):
    return jax.shard_map(
        per_device,
        mesh=mesh,
        in_specs=(P("mem", "pts", None), P(), P(), P(None, "pts"), P("pts"), P(), P("pts")),
        out_specs=(P("mem", "pts", None), P(), P()),
        check_vma=False,
    )
```

profile of v0, /device:TPU:1, one launch (start us, length us, event | category | flops | bytes accessed | tf_op | source)
XLA Modules:
  0.0 54.7 jit_solution(9251226698968987097)
XLA Ops:
  0.6 50.6 %shard_map.94 = (bf16[2,2048,1024]{2,1,0:T(8,128)(2,1)S(1)}, bf16[56,16,128]{2,1,0:T(8,128)(2,1)S(1)}) custom-call(bf16[2,2048,1024]{2,1,0:T(8,128)(2,1)} %latent.1, bf16[102,1024]{1,0:T(8,128)(2,1)} %w_hbm.1, bf16[1,102]{1,0:T(2,128)(2,1)} %bitcast.7, s32[1,102]{1,0:T(1,128)} %bitcast.8, f32[102,2048]{1,0:T(8,128)} %tgt.1, f32[1,2048]{1,0:T(1,128)} %bitcast.5, ...), custom_call_target="tpu_custom_call" | custom-call | tf_op jit(solution)/shard_map/pallas_call | solution.py:571
  51.2 3.5 %shard_map.95 = (bf16[2,2048,1024]{2,1,0:T(8,128)(2,1)}, f32[102,1024]{1,0:T(8,128)}, f32[1,102]{1,0:T(1,128)}) custom-call(bf16[2,2048,1024]{2,1,0:T(8,128)(2,1)S(1)} %get-tuple-element.8.lg, bf16[56,16,128]{2,1,0:T(8,128)(2,1)S(1)} %get-tuple-element.9.ag), custom_call_target="tpu_custom_call" | custom-call | tf_op jit(solution)/shard_map/pallas_call | solution.py:622
where the time goes:
time: 54.8 us; the launch traced here: 54.7 us
  Pallas kernels  54 us (99%)
  between operations  0.64 us (1%)
    pallas_call x1, Pallas kernels, per_device(): pl.pallas_call(main_kernel, out_shape=(pltpu.VMEM((2, SLOTS, L), bf16), p...  50.6 us
    pallas_call x1, Pallas kernels, per_device(): pl.pallas_call(output_kernel, in_specs=[vmem, vmem], out_specs=(hbm, hbm,...  3.49 us

commit v1 on v0

--- a/solution.py
+++ b/solution.py
@@ -24,6 +24,7 @@
 CHIPS = 64
 VMEM = 40 * 2**20
 EARLY = 2
+SUMS = (((0, 0),), ((0, 1), (1, 0)), (), ((1, 1), (0, 2), (1, 2), (0, 3), (1, 3)))
 ORDER = (0, 2, 1, 3)
 MESH = pl.DeviceIdType.MESH
 
@@ -346,7 +347,7 @@
                     sp[n, pl.ds(pl.multiple_of(16 * t, 16), 16), at : at + 128] = sums[n]
                 return 0
 
-            lax.fori_loop(0, MAIN // 16, step, 0)
+            lax.fori_loop(0, MAIN // 16, step, 0, unroll=3)
             sums = pair_sums(rest_rows(near_buffers(k), lanes), rest_rows(far_buffers(k), lanes))
             for n in range(4):
                 sp[n, MAIN:FP, at : at + 128] = sums[n]
@@ -368,7 +369,7 @@
                 bsum[rows, :] += sum(grad.astype(jnp.float32) for grad in grads)
                 return 0
 
-            lax.fori_loop(0, MAIN // 16, step, 0)
+            lax.fori_loop(0, MAIN // 16, step, 0, unroll=3)
             grads = grads_of(rest_rows(near_buffers(k), lanes), slice(MAIN, FP))
             none = jnp.zeros((8, 128), jnp.float32)
             for n in range(4):
@@ -414,12 +415,10 @@
             pairs_chunk(k)
         grads_chunk(k)
         grad_copy(k).start()
-        accumulate(0, k)
-        if k > 0:
-            grad_copy(k - 1).wait_recv()
-            accumulate(1, k - 1)
-    grad_copy(NK - 1).wait_recv()
-    accumulate(1, NK - 1)
+        for e, done in SUMS[k]:
+            if e == 1:
+                grad_copy(done).wait_recv()
+            accumulate(e, done)
 
     at = lax.broadcasted_iota(jnp.int32, (FP, 128), 0)
     lane_at = lax.broadcasted_iota(jnp.int32, (FP, 128), 1)

time: 54.8 us -> 54.6 us (level)
  no operation moved by 1% of the time
where the time goes in v1:
time: 54.6 us; the launch traced here: 54.5 us
  Pallas kernels  53.9 us (99%)
  between operations  0.64 us (1%)
    pallas_call x1, Pallas kernels, per_device(): pl.pallas_call(main_kernel, out_shape=(pltpu.VMEM((2, SLOTS, L), bf16), p...  50.4 us
    pallas_call x1, Pallas kernels, per_device(): pl.pallas_call(output_kernel, in_specs=[vmem, vmem], out_specs=(hbm, hbm,...  3.49 us

profile of v1, /device:TPU:1, one launch (start us, length us, event | category | flops | bytes accessed | tf_op | source)
XLA Modules:
  0.0 54.5 jit_solution(7173324565282523887)
XLA Ops:
  0.6 50.4 %shard_map.94 = (bf16[2,2048,1024]{2,1,0:T(8,128)(2,1)S(1)}, bf16[56,16,128]{2,1,0:T(8,128)(2,1)S(1)}) custom-call(bf16[2,2048,1024]{2,1,0:T(8,128)(2,1)} %latent.1, bf16[102,1024]{1,0:T(8,128)(2,1)} %w_hbm.1, bf16[1,102]{1,0:T(2,128)(2,1)} %bitcast.7, s32[1,102]{1,0:T(1,128)} %bitcast.8, f32[102,2048]{1,0:T(8,128)} %tgt.1, f32[1,2048]{1,0:T(1,128)} %bitcast.5, ...), custom_call_target="tpu_custom_call" | custom-call | tf_op jit(solution)/shard_map/pallas_call | solution.py:570
  51.0 3.5 %shard_map.95 = (bf16[2,2048,1024]{2,1,0:T(8,128)(2,1)}, f32[102,1024]{1,0:T(8,128)}, f32[1,102]{1,0:T(1,128)}) custom-call(bf16[2,2048,1024]{2,1,0:T(8,128)(2,1)S(1)} %get-tuple-element.8.lg, bf16[56,16,128]{2,1,0:T(8,128)(2,1)S(1)} %get-tuple-element.9.ag), custom_call_target="tpu_custom_call" | custom-call | tf_op jit(solution)/shard_map/pallas_call | solution.py:621

commit v2 on v1

--- a/solution.py
+++ b/solution.py
@@ -347,7 +347,7 @@
                     sp[n, pl.ds(pl.multiple_of(16 * t, 16), 16), at : at + 128] = sums[n]
                 return 0
 
-            lax.fori_loop(0, MAIN // 16, step, 0, unroll=3)
+            lax.fori_loop(0, MAIN // 16, step, 0, unroll=6)
             sums = pair_sums(rest_rows(near_buffers(k), lanes), rest_rows(far_buffers(k), lanes))
             for n in range(4):
                 sp[n, MAIN:FP, at : at + 128] = sums[n]
@@ -369,7 +369,7 @@
                 bsum[rows, :] += sum(grad.astype(jnp.float32) for grad in grads)
                 return 0
 
-            lax.fori_loop(0, MAIN // 16, step, 0, unroll=3)
+            lax.fori_loop(0, MAIN // 16, step, 0, unroll=6)
             grads = grads_of(rest_rows(near_buffers(k), lanes), slice(MAIN, FP))
             none = jnp.zeros((8, 128), jnp.float32)
             for n in range(4):

time: 54.6 us -> 54.5 us (level)
  no operation moved by 1% of the time
where the time goes in v2:
time: 54.5 us; the launch traced here: 54.4 us
  Pallas kernels  53.8 us (99%)
  between operations  0.64 us (1%)
    pallas_call x1, Pallas kernels, per_device(): pl.pallas_call(main_kernel, out_shape=(pltpu.VMEM((2, SLOTS, L), bf16), p...  50.3 us
    pallas_call x1, Pallas kernels, per_device(): pl.pallas_call(output_kernel, in_specs=[vmem, vmem], out_specs=(hbm, hbm,...  3.49 us

profile of v2, /device:TPU:1, one launch (start us, length us, event | category | flops | bytes accessed | tf_op | source)
XLA Modules:
  0.0 54.4 jit_solution(16925335213039235914)
XLA Ops:
  0.6 50.3 %shard_map.94 = (bf16[2,2048,1024]{2,1,0:T(8,128)(2,1)S(1)}, bf16[56,16,128]{2,1,0:T(8,128)(2,1)S(1)}) custom-call(bf16[2,2048,1024]{2,1,0:T(8,128)(2,1)} %latent.1, bf16[102,1024]{1,0:T(8,128)(2,1)} %w_hbm.1, bf16[1,102]{1,0:T(2,128)(2,1)} %bitcast.7, s32[1,102]{1,0:T(1,128)} %bitcast.8, f32[102,2048]{1,0:T(8,128)} %tgt.1, f32[1,2048]{1,0:T(1,128)} %bitcast.5, ...), custom_call_target="tpu_custom_call" | custom-call | tf_op jit(solution)/shard_map/pallas_call | solution.py:570
  50.9 3.5 %shard_map.95 = (bf16[2,2048,1024]{2,1,0:T(8,128)(2,1)}, f32[102,1024]{1,0:T(8,128)}, f32[1,102]{1,0:T(1,128)}) custom-call(bf16[2,2048,1024]{2,1,0:T(8,128)(2,1)S(1)} %get-tuple-element.8.lg, bf16[56,16,128]{2,1,0:T(8,128)(2,1)S(1)} %get-tuple-element.9.ag), custom_call_target="tpu_custom_call" | custom-call | tf_op jit(solution)/shard_map/pallas_call | solution.py:621
